TPU v7x, 256 devices: a whole 4x4x8 slice. The times are simulated.
256 devices in a mesh: replica: 16 (over z, core), mp: 16 (over y, x).
Axes of the slice: x: 4, y: 4, z: 8, core: 2. Of those that a mesh axis runs over, the one named last changes fastest.
Arguments:
- pre_act: bfloat16 [2400, 32768], P('mp', 'replica'), may hold values from -6 to 6
- out_grad: bfloat16 [32768, 4800], P(('replica', 'mp')), may hold values from -6 to 6
- weight: bfloat16 [2400, 4800], P('mp'), may hold values from -0.09375 to 0.09375
- error: float32 [16, 2400, 4800], P('replica', 'mp'), may hold values from -96 to 96
- q_init: float32 [4800, 32], replicated, may hold values from -6 to 6
Outputs:
- pre_grad: bfloat16 [2400, 32768], P('mp', 'replica')
- new_error: float32 [16, 2400, 4800], P('replica', 'mp')
- q_new: float32 [4800, 32], replicated
All inputs are finite; a program needn't handle non-finite values.
Results may differ from a plain program's by a relative error of at most 0.013.
Values may be sent and summed in bfloat16 or wider, within the bound.
No kernel may reach another device: no remote copies, remote signals or barrier semaphores. Data moves between devices by JAX's collectives and lax.ppermute only.
A program may use at most 128 MiB of HBM per device.

v0:
```python
import jax
import jax.numpy as jnp
from jax import lax
from jax.sharding import PartitionSpec as P

F32 = jnp.float32
BF16 = jnp.bfloat16


def gelu_back(pre, grad):
    _, pull = jax.vjp(jax.nn.gelu, pre)
    return pull(grad)[0]


def gelu16(pre):
    return jax.nn.gelu(pre.astype(F32)).astype(BF16)


def split(x, parts):
    out = []
    for _ in range(parts):
        top = lax.reduce_precision(x, 8, 7)
        out.append(top.astype(BF16))
        x = x - top
    return out


def dot(a, b, ca, cb):
    return lax.dot_general(a, b, (((ca,), (cb,)), ((), ())), preferred_element_type=F32)


def fold(x, parts, axis=0):
    n = x.shape[axis] // parts
    return sum((lax.slice_in_dim(x, i * n, (i + 1) * n, axis=axis) for i in range(parts)))


def spread(x, axis):
    n = lax.axis_size(axis)
    return lax.all_to_all(jnp.broadcast_to(x, (n,) + x.shape), axis, 0, 0, tiled=True)


def shards(pre_act, out_grad, weight, error, q_init):
    hi = lax.Precision.HIGHEST
    groups = lax.axis_size("replica")
    mp = lax.axis_size("mp")
    rank = q_init.shape[1]
    hid, toks = pre_act.shape
    own, feat = out_grad.shape
    error = error[0]
    cut = feat // 256 * 128
    blocks = [(0, cut), (cut, feat)]
    pieces = [lax.all_gather(out_grad[:, lo:up], "mp", axis=0, tiled=True) for lo, up in blocks]
    q3 = jnp.concatenate(split(q_init, 3), axis=1)
    y = fold(dot(q3, out_grad, 0, 1), 3)
    y3 = jnp.concatenate(split(y, 3), axis=0)
    mine = pre_act.reshape(hid, mp, own).transpose(1, 0, 2)
    room = -(-hid // 16) * 16
    sent = jnp.concatenate(
        [mine, jnp.zeros((mp, room - hid, own), BF16), jnp.broadcast_to(y3, (mp,) + y3.shape)],
        axis=1,
    )
    got = lax.all_to_all(sent, "mp", 0, 0, tiled=True)
    act_own = gelu16(got[:, :hid])
    y_all = got[:, room:].transpose(1, 0, 2).reshape(3 * rank, toks)
    act = gelu16(pre_act)
    e2 = split(error, 2)
    p_err = sum((fold(dot(q3, e, 0, 1), 3) for e in e2))
    p_local = fold(dot(y_all, act, 1, 1), 3) + p_err
    pbar = jnp.sum(spread(p_local, "replica"), axis=0) / groups
    p_all = spread(pbar, "mp")
    gram = jnp.einsum("mih,mjh->ij", p_all, p_all, precision=hi)
    lower = jnp.linalg.cholesky(gram)
    inv = jax.scipy.linalg.solve_triangular(lower, jnp.eye(rank, dtype=F32), lower=True)
    p3 = jnp.concatenate(split(p_all, 3), axis=1)
    z = fold(
        lax.dot_general(p3, act_own, (((2,), (1,)), ((0,), (0,))), preferred_element_type=F32).sum(
            0
        ),
        3,
    )
    z3 = jnp.concatenate(split(z, 3), axis=0)
    l3 = jnp.concatenate(split(pbar, 3), axis=0)
    r_local = fold(dot(z3, out_grad, 1, 0), 3) + sum((fold(dot(l3, e, 1, 0), 3) for e in e2))
    rows = r_local.reshape(mp, rank // mp, feat)
    r_part = jnp.sum(lax.all_to_all(rows, "mp", 0, 0, tiled=True), axis=0)
    r_part = jnp.sum(spread(r_part, "replica"), axis=0) / groups
    r_all = spread(r_part, "mp").reshape(rank, feat)
    q_t = jnp.dot(inv, r_all, precision=hi)
    phat = jnp.dot(inv, pbar, precision=hi)
    ph, pl = split(phat, 2)
    qh, ql = split(q_t, 2)
    left = jnp.concatenate([ph, ph, pl], axis=0)
    right = jnp.concatenate([qh, ql, qh], axis=0)
    back = 0.0
    errs = []
    for (lo, up), piece in zip(blocks, pieces):
        back = back + dot(weight[:, lo:up], piece, 1, 1)
        mat = dot(act, piece, 1, 0) + error[:, lo:up]
        errs.append(mat - dot(left, right[:, lo:up], 0, 0))
    pre_grad = gelu_back(pre_act.astype(F32), back).astype(BF16)
    new_error = jnp.concatenate(errs, axis=1)[None]
    return (pre_grad, new_error, q_t.T)


def solution(mesh):
    return jax.shard_map(
        shards,
        mesh=mesh,
        in_specs=(
            P("mp", "replica"),
            P(("replica", "mp"), None),
            P("mp", None),
            P("replica", "mp", None),
            P(),
        ),
        out_specs=(P("mp", "replica"), P("replica", "mp", None), P()),
        check_vma=False,
    )
```

profile of v0, /device:TPU:1, one launch (start us, length us, event | category | flops | bytes accessed | tf_op | source)
XLA Modules:
  0.0 246.4 jit_solution(8934448072027616238)
XLA Ops:
  7.2 2.0 slice.115
  9.3 0.9 slice.117
  10.9 0.4 fusion.85
  11.3 0.3 copy-done.12
  11.9 0.3 pad_maximum_fusion
  12.3 1.2 copy.35
  13.5 7.8 %all-to-all-start = ((bf16[16,256,128]{2,1,0:T(8,128)(2,1)}), bf16[16,256,128]{2,1,0:T(8,128)(2,1)}, u32[]{:S(2)}, u32[]{:S(2)}) async-start(bf16[16,256,128]{2,1,0:T(8,128)(2,1)} %copy.35), calls=%async_computation | async-start | bytes 2097152 | tf_op jit(solution)/shard_map/all_to_all | solution.py:62
  21.3 1.7 fusion.38
  23.0 0.6 fusion.52
  23.6 16.9 %all-to-all-done = bf16[16,256,128]{2,1,0:T(8,128)(2,1)} async-done(((bf16[16,256,128]{2,1,0:T(8,128)(2,1)}), bf16[16,256,128]{2,1,0:T(8,128)(2,1)}, u32[]{:S(2)}, u32[]{:S(2)}) %all-to-all-start) | async-done | bytes 1048608 | tf_op jit(solution)/shard_map/all_to_all | solution.py:62
  40.5 1.8 fusion.47
  42.6 29.8 %all_to_all.30 = f32[16,32,150]{2,1,0:T(8,128)S(1)} all-to-all(f32[16,32,150]{2,1,0:T(8,128)S(1)} %broadcast_in_dim.25), channel_id=1, replica_groups=mesh['replica'=16,'mp'=16] {'replica'}, dimensions={0} | all-to-all | bytes 614400 | tf_op jit(solution)/shard_map/all_to_all | solution.py:39
  72.5 0.8 broadcast_in_dim.26
  73.3 3.6 %all-to-all-start.2 = ((f32[16,32,150]{2,1,0:T(8,128)}), f32[16,32,150]{2,1,0:T(8,128)S(1)}, u32[]{:S(2)}, u32[]{:S(2)}) async-start(f32[16,32,150]{2,1,0:T(8,128)} %broadcast_in_dim.26), calls=%async_computation.2 | async-start | bytes 1048576 | tf_op jit(solution)/shard_map/all_to_all | solution.py:39
  76.9 1.7 fusion.50
  78.7 1.8 fusion.37
  80.4 12.7 %all-to-all-done.2 = f32[16,32,150]{2,1,0:T(8,128)S(1)} async-done(((f32[16,32,150]{2,1,0:T(8,128)}), f32[16,32,150]{2,1,0:T(8,128)S(1)}, u32[]{:S(2)}, u32[]{:S(2)}) %all-to-all-start.2) | async-done | bytes 307232 | tf_op jit(solution)/shard_map/all_to_all | solution.py:39
  93.3 2.0 convolution_bitcast_fusion
  95.3 0.5 fusion.60
  95.8 1.0 copy-done.2
  96.8 1.1 fusion.31
  97.9 2.3 reshape.30
  100.1 21.9 %all_to_all.31 = f32[16,2,4800]{2,1,0:T(2,128)} all-to-all(f32[16,2,4800]{2,1,0:T(2,128)} %reshape.30), channel_id=1, replica_groups=mesh['replica'=16,'mp'=16] {'mp'}, dimensions={0} | all-to-all | bytes 1228800 | tf_op jit(solution)/shard_map/all_to_all | solution.py:85
  122.1 1.3 reduce_sum.32
  123.4 1.0 broadcast_in_dim.27
  124.4 4.4 %all-to-all-start.4 = ((f32[16,2,4800]{2,1,0:T(2,128)}), f32[16,2,4800]{2,1,0:T(2,128)}, u32[]{:S(2)}, u32[]{:S(2)}) async-start(f32[16,2,4800]{2,1,0:T(2,128)} %broadcast_in_dim.27), calls=%async_computation.4 | async-start | bytes 1245184 | tf_op jit(solution)/shard_map/all_to_all | solution.py:39
  128.7 1.8 copy.64
  130.5 0.6 convolution_bitcast_fusion.1
  131.2 2.9 %cholesky.17 = f32[32,32]{1,0:T(8,128)S(1)} custom-call(f32[32,32]{1,0:T(8,128)S(1)} %fusion.73), custom_call_target="Cholesky" | custom-call | tf_op jit(solution)/shard_map/jit(cholesky)/cholesky | solution.py:72
  134.1 0.6 compare_reduce_fusion
  134.8 13.4 %all-to-all-done.4 = f32[16,2,4800]{2,1,0:T(2,128)} async-done(((f32[16,2,4800]{2,1,0:T(2,128)}), f32[16,2,4800]{2,1,0:T(2,128)}, u32[]{:S(2)}, u32[]{:S(2)}) %all-to-all-start.4) | async-done | bytes 614432 | tf_op jit(solution)/shard_map/all_to_all | solution.py:39
  148.2 1.3 reduce_sum.33
  149.5 1.0 broadcast_in_dim.28
  150.4 3.8 %all-to-all-start.5 = ((f32[16,2,4800]{2,1,0:T(2,128)}), f32[16,2,4800]{2,1,0:T(2,128)S(1)}, u32[]{:S(2)}, u32[]{:S(2)}) async-start(f32[16,2,4800]{2,1,0:T(2,128)} %broadcast_in_dim.28), calls=%async_computation.5 | async-start | bytes 1245184 | tf_op jit(solution)/shard_map/all_to_all | solution.py:39
  154.2 0.7 fusion.66
  154.9 2.4 custom-call.7
  157.7 8.3 %all-to-all-done.5 = f32[16,2,4800]{2,1,0:T(2,128)S(1)} async-done(((f32[16,2,4800]{2,1,0:T(2,128)}), f32[16,2,4800]{2,1,0:T(2,128)S(1)}, u32[]{:S(2)}, u32[]{:S(2)}) %all-to-all-start.5) | async-done | bytes 614432 | tf_op jit(solution)/shard_map/all_to_all | solution.py:39
  166.1 0.4 reshape.31
  166.5 1.5 fusion.29
  168.0 7.6 %convolution_add_fusion = f32[150,2304]{1,0:T(8,128)S(1)} fusion(bf16[2048,2304]{0,1:T(8,128)(2,1)} %all-gather.3.cloned.1.call-done, f32[150,4800]{1,0:T(8,128)} %bitcast.55, bf16[150,2048]{1,0:T(8,128)(2,1)S(1)} %copy-done.10), kind=kOutput, calls=%fused_computation.4 | convolution fusion | flops 1418995200 | bytes 12816384 | tf_op jit(solution)/shard_map/dot_general | solution.py:29
  175.6 0.4 convolution_subtract_fusion
  176.0 1.0 copy-done.6
  177.0 1.7 fusion.24
  178.7 43.7 %all-gather.5.cloned.1.call-done = bf16[2048,2496]{0,1:T(8,128)(2,1)} async-done(((bf16[128,2496]{0,1:T(8,128)(2,1)}), bf16[2048,2496]{0,1:T(8,128)(2,1)}) %all-gather.5.cloned.1.call-update) | async-done | bytes 10223632 | tf_op jit(solution)/shard_map/all_gather | solution.py:52
  222.4 8.1 %convolution_add_fusion.1 = f32[150,2496]{1,0:T(8,128)S(1)} fusion(bf16[2048,2496]{0,1:T(8,128)(2,1)} %all-gather.5.cloned.1.call-done, f32[150,4800]{1,0:T(8,128)} %bitcast.56, bf16[150,2048]{1,0:T(8,128)(2,1)} %param.5), kind=kOutput, calls=%fused_computation.5 | convolution fusion | flops 1536988800 | bytes 13833216 | tf_op jit(solution)/shard_map/dot_general | solution.py:29
  230.6 0.4 convolution_subtract_fusion.1
  231.2 4.6 %copy.41 = f32[1,150,4800]{2,0,1:T(1,128)} copy(f32[1,150,4800]{2,1,0:T(8,128)S(1)} %maximum_bitcast_fusion) | data formatting | bytes 5760000
  235.8 3.7 %fusion.5 = bf16[150,2048]{1,0:T(8,128)(2,1)} fusion(bf16[150,2048]{1,0:T(8,128)(2,1)S(1)} %copy-done.11, f32[150,2048]{1,0:T(8,128)S(1)} %fusion.24, bf16[2048,2496]{0,1:T(8,128)(2,1)S(1)} %bitcast.61, bf16[150,4800]{1,0:T(8,128)(2,1)S(1)} %copy-done.7), kind=kOutput, calls=%fused_computation.23 | convolution fusion | flops 1540300800 | bytes 13484032 | tf_op jit(solution)/shard_map/dot_general | solution.py:29
  (65 shorter events, 2.3 us)
Async XLA Ops:
  7.2 2.2 copy-start.4
  7.2 160.8 %all-gather.3.cloned.1.call-start = ((), (), s32[]{:S(2)}) async-start(), calls=%async_computation.6 | async-start | bytes 10027008 | tf_op jit(solution)/shard_map/all_gather | solution.py:52
  9.2 1.1 copy-start.9
  9.3 1.5 copy-start.8
  9.3 213.1 %all-gather.5.cloned.1.call-start = ((), (), s32[]{:S(2)}) async-start(), calls=%async_computation.7 | async-start | bytes 10862592 | tf_op jit(solution)/shard_map/all_gather | solution.py:52
  10.9 0.7 copy-start.12
  10.9 0.8 copy-start.14
  12.3 9.0 %copy-start = (f32[1,150,4800]{2,0,1:T(1,128)S(1)}, f32[1,150,4800]{2,0,1:T(1,128)}, u32[]{:S(2)}) copy-start(f32[1,150,4800]{2,0,1:T(1,128)} %param.8) | copy-start | bytes 8640004
  13.5 27.0 %all-to-all-start = ((bf16[16,256,128]{2,1,0:T(8,128)(2,1)}), bf16[16,256,128]{2,1,0:T(8,128)(2,1)}, u32[]{:S(2)}, u32[]{:S(2)}) async-start(bf16[16,256,128]{2,1,0:T(8,128)(2,1)} %copy.35), calls=%async_computation | async-start | bytes 2097152 | tf_op jit(solution)/shard_map/all_to_all | solution.py:62
  21.3 1.7 copy-start.13
  21.3 1.7 copy-start.15
  73.3 19.8 %all-to-all-start.2 = ((f32[16,32,150]{2,1,0:T(8,128)}), f32[16,32,150]{2,1,0:T(8,128)S(1)}, u32[]{:S(2)}, u32[]{:S(2)}) async-start(f32[16,32,150]{2,1,0:T(8,128)} %broadcast_in_dim.26), calls=%async_computation.2 | async-start | bytes 1048576 | tf_op jit(solution)/shard_map/all_to_all | solution.py:39
  93.3 2.0 copy-start.5
  93.3 2.6 %copy-start.3 = (f32[96,4800]{1,0:T(8,128)S(1)}, f32[96,4800]{1,0:T(8,128)}, u32[]{:S(2)}) copy-start(f32[96,4800]{1,0:T(8,128)} %fusion.37) | copy-start | bytes 5529604
  95.3 1.5 copy-start.2
  124.4 23.8 %all-to-all-start.4 = ((f32[16,2,4800]{2,1,0:T(2,128)}), f32[16,2,4800]{2,1,0:T(2,128)}, u32[]{:S(2)}, u32[]{:S(2)}) async-start(f32[16,2,4800]{2,1,0:T(2,128)} %broadcast_in_dim.27), calls=%async_computation.4 | async-start | bytes 1245184 | tf_op jit(solution)/shard_map/all_to_all | solution.py:39
  150.4 15.6 %all-to-all-start.5 = ((f32[16,2,4800]{2,1,0:T(2,128)}), f32[16,2,4800]{2,1,0:T(2,128)S(1)}, u32[]{:S(2)}, u32[]{:S(2)}) async-start(f32[16,2,4800]{2,1,0:T(2,128)} %broadcast_in_dim.28), calls=%async_computation.5 | async-start | bytes 1245184 | tf_op jit(solution)/shard_map/all_to_all | solution.py:39
  157.7 10.3 %copy-start.10 = (bf16[150,2048]{1,0:T(8,128)(2,1)S(1)}, bf16[150,2048]{1,0:T(8,128)(2,1)}, u32[]{:S(2)}) copy-start(bf16[150,2048]{1,0:T(8,128)(2,1)} %param.5) | copy-start | bytes 1843204
  168.0 8.0 %copy-start.1 = (bf16[2048,2304]{0,1:T(8,128)(2,1)S(1)}, bf16[2048,2304]{0,1:T(8,128)(2,1)}, u32[]{:S(2)}) copy-start(bf16[2048,2304]{0,1:T(8,128)(2,1)} %all-gather.3.cloned.1.call-done) | copy-start | bytes 28311556
  175.6 1.4 copy-start.6
  222.4 13.4 %slice-start = ((s8[10223616]{0:T(1024)(128)(4,1)}), s8[4194304]{0:T(1024)(128)(4,1)S(1)}, s32[]{:S(2)}) async-start(s8[10223616]{0:T(1024)(128)(4,1)} %bitcast.60), calls=%async_computation.8 | async-start | bytes 8388608
  222.4 13.4 %slice-start.1 = ((s8[10223616]{0:T(1024)(128)(4,1)}), s8[4194304]{0:T(1024)(128)(4,1)S(1)}, s32[]{:S(2)}) async-start(s8[10223616]{0:T(1024)(128)(4,1)} %bitcast.60), calls=%async_computation.9 | async-start | bytes 8388608
  231.0 4.8 %slice-start.2 = ((s8[10223616]{0:T(1024)(128)(4,1)}), s8[1835008]{0:T(1024)(128)(4,1)S(1)}, s32[]{:S(2)}) async-start(s8[10223616]{0:T(1024)(128)(4,1)} %bitcast.60), calls=%async_computation.10 | async-start | bytes 3670016
  231.2 4.6 %copy-start.7 = (bf16[150,4800]{1,0:T(8,128)(2,1)S(1)}, bf16[150,4800]{1,0:T(8,128)(2,1)}, u32[]{:S(2)}) copy-start(bf16[150,4800]{1,0:T(8,128)(2,1)} %param.7) | copy-start | bytes 4320004
  231.2 4.6 %copy-start.11 = (bf16[150,2048]{1,0:T(8,128)(2,1)S(1)}, bf16[150,2048]{1,0:T(8,128)(2,1)}, u32[]{:S(2)}) copy-start(bf16[150,2048]{1,0:T(8,128)(2,1)} %param.5) | copy-start | bytes 1843204
Sparse Core Ops, SparseCore 0:
  10.4 111.0 all-gather.2
  124.0 98.4 all-gather.4
where the time goes:
time: 247 us; the launch traced here: 246 us
  waiting for transfers between devices  95 us (38%)
  blocking collectives  51.8 us (21%)
  matrix products  34.8 us (14%)
  starting transfers between devices  19.6 us (8%)
  local copies, waits for them, and re-layouts  19.4 us (8%)
  between operations  14.5 us (6%)
  other arithmetic  11.4 us (5%)
    all_gather x2, waiting for transfers between devices, shards(): lax.all_gather(out_grad[:, lo:up], 'mp', axis=0, tiled=True)  43.7 us
    all_to_all x3, waiting for transfers between devices, spread(): lax.all_to_all(jnp.broadcast_to(x, (n,) + x.shape), axis, 0, 0, tiled=True)  34.4 us
    dot_general x13, matrix products, dot(): lax.dot_general(a, b, (((ca,), (cb,)), ((), ())), preferred_element_type=...  30.4 us
    all_to_all x1, blocking collectives, spread(): lax.all_to_all(jnp.broadcast_to(x, (n,) + x.shape), axis, 0, 0, tiled=True)  29.8 us
    all_to_all x1, blocking collectives, shards(): r_part = jnp.sum(lax.all_to_all(rows, 'mp', 0, 0, tiled=True), axis=0)  21.9 us
    all_to_all x1, waiting for transfers between devices, shards(): got = lax.all_to_all(sent, 'mp', 0, 0, tiled=True)  16.9 us
    all_to_all x3, starting transfers between devices, spread(): lax.all_to_all(jnp.broadcast_to(x, (n,) + x.shape), axis, 0, 0, tiled=True)  11.7 us
    unnamed x41, local copies, waits for them, and re-layouts  9.28 us
  transfers between devices with their start and end apart: 6, of which 5 were waited for; matrix products, arithmetic and copies ran while one was open for 18% of the time, Pallas kernels for 0%

commit v1 on v0

--- a/solution.py
+++ b/solution.py
@@ -49,7 +49,13 @@
     error = error[0]
     cut = feat // 256 * 128
     blocks = [(0, cut), (cut, feat)]
-    pieces = [lax.all_gather(out_grad[:, lo:up], "mp", axis=0, tiled=True) for lo, up in blocks]
+    pieces = [
+        jnp.concatenate(
+            lax.all_to_all(jnp.stack([out_grad[:, lo:up]] * lax.axis_size("mp")), "mp", 0, 0),
+            axis=0,
+        )
+        for lo, up in blocks
+    ]
     q3 = jnp.concatenate(split(q_init, 3), axis=1)
     y = fold(dot(q3, out_grad, 0, 1), 3)
     y3 = jnp.concatenate(split(y, 3), axis=0)

time: 247 us -> 490 us (1.98)
  waiting for transfers between devices: 95 us -> 291 us
  local copies, waits for them, and re-layouts: 19.4 us -> 51.1 us
  blocking collectives: 51.8 us -> 68.9 us
  between operations: 14.5 us -> 1.08 us
  starting transfers between devices: 19.6 us -> 25.4 us
    all_to_all x0 -> x2, waiting for transfers between devices: none -> 261 us  [shards(): lax.all_to_all(jnp.stack([out_grad[:, lo:up]] * lax.axis_size('mp')), 'mp...]
    all_gather x2 -> x0, waiting for transfers between devices: 43.7 us -> none  [shards(): lax.all_gather(out_grad[:, lo:up], 'mp', axis=0, tiled=True)]
    all_to_all x1 -> x2, blocking collectives: 29.8 us -> 51.9 us  [spread(): lax.all_to_all(jnp.broadcast_to(x, (n,) + x.shape), axis, 0, 0, tiled=True)]
    all_to_all x3 -> x2, waiting for transfers between devices: 34.4 us -> 16.7 us  [spread(): lax.all_to_all(jnp.broadcast_to(x, (n,) + x.shape), axis, 0, 0, tiled=True)]
    all_to_all x0 -> x1, local copies, waits for them, and re-layouts: none -> 13.7 us  [shards(): lax.all_to_all(jnp.stack([out_grad[:, lo:up]] * lax.axis_size('mp')), 'mp...]
    another operation x0 -> x2, local copies, waits for them, and re-layouts: none -> 12.6 us  [shards(): jnp.stack([out_grad[:, lo:up]] * lax.axis_size('mp'))]
    all_to_all x0 -> x2, starting transfers between devices: none -> 9.8 us  [shards(): lax.all_to_all(jnp.stack([out_grad[:, lo:up]] * lax.axis_size('mp')), 'mp...]
    all_to_all x1, blocking collectives: 21.9 us -> 17 us  [shards(): r_part = jnp.sum(lax.all_to_all(rows, 'mp', 0, 0, tiled=True), axis=0)]
  transfers between devices with their start and end apart: 6 -> 5, of which waited for: 5 -> 5; matrix products, arithmetic and copies ran while one was open for 18% -> 8% of each run, Pallas kernels for 0% -> 0%
where the time goes in v1:
time: 490 us; the launch traced here: 487 us
  waiting for transfers between devices  291 us (59%)
  blocking collectives  68.9 us (14%)
  local copies, waits for them, and re-layouts  51.1 us (10%)
  matrix products  38 us (8%)
  starting transfers between devices  25.4 us (5%)
  other arithmetic  11.4 us (2%)
    all_to_all x2, waiting for transfers between devices, shards(): lax.all_to_all(jnp.stack([out_grad[:, lo:up]] * lax.axis_size('mp')), 'mp...  261 us
    all_to_all x2, blocking collectives, spread(): lax.all_to_all(jnp.broadcast_to(x, (n,) + x.shape), axis, 0, 0, tiled=True)  51.9 us
    dot_general x13, matrix products, dot(): lax.dot_general(a, b, (((ca,), (cb,)), ((), ())), preferred_element_type=...  33.6 us
    all_to_all x1, blocking collectives, shards(): r_part = jnp.sum(lax.all_to_all(rows, 'mp', 0, 0, tiled=True), axis=0)  17 us
    all_to_all x2, waiting for transfers between devices, spread(): lax.all_to_all(jnp.broadcast_to(x, (n,) + x.shape), axis, 0, 0, tiled=True)  16.7 us
    all_to_all x1, waiting for transfers between devices, shards(): got = lax.all_to_all(sent, 'mp', 0, 0, tiled=True)  13.7 us
    all_to_all x1, local copies, waits for them, and re-layouts, shards(): lax.all_to_all(jnp.stack([out_grad[:, lo:up]] * lax.axis_size('mp')), 'mp...  13.7 us
    another operation x2, local copies, waits for them, and re-layouts, shards(): jnp.stack([out_grad[:, lo:up]] * lax.axis_size('mp'))  12.6 us
  transfers between devices with their start and end apart: 5, of which 5 were waited for; matrix products, arithmetic and copies ran while one was open for 8% of the time, Pallas kernels for 0%

profile of v1, /device:TPU:1, one launch (start us, length us, event | category | flops | bytes accessed | tf_op | source)
XLA Modules:
  0.0 487.2 jit_solution(7106130010945643451)
XLA Ops:
  0.6 1.3 copy.57
  2.2 1.2 copy-done.4
  4.4 1.2 copy.46
  5.6 7.8 %all-to-all-start.2 = ((bf16[16,256,128]{2,1,0:T(8,128)(2,1)}), bf16[16,256,128]{2,1,0:T(8,128)(2,1)}, u32[]{:S(2)}, u32[]{:S(2)}) async-start(bf16[16,256,128]{2,1,0:T(8,128)(2,1)} %copy.46), calls=%async_computation.2 | async-start | bytes 2097152 | tf_op jit(solution)/shard_map/all_to_all | solution.py:68
  13.4 1.7 fusion.38
  15.1 0.6 fusion.52
  15.7 13.7 %all-to-all-done.2 = bf16[16,256,128]{2,1,0:T(8,128)(2,1)} async-done(((bf16[16,256,128]{2,1,0:T(8,128)(2,1)}), bf16[16,256,128]{2,1,0:T(8,128)(2,1)}, u32[]{:S(2)}, u32[]{:S(2)}) %all-to-all-start.2) | async-done | bytes 1048608 | tf_op jit(solution)/shard_map/all_to_all | solution.py:68
  29.5 1.8 fusion.47
  31.6 28.2 %all_to_all.40 = f32[16,32,150]{2,1,0:T(8,128)S(1)} all-to-all(f32[16,32,150]{2,1,0:T(8,128)S(1)} %broadcast_in_dim.25), channel_id=1, replica_groups=mesh['replica'=16,'mp'=16] {'replica'}, dimensions={0} | all-to-all | bytes 614400 | tf_op jit(solution)/shard_map/all_to_all | solution.py:39
  59.8 0.8 broadcast_in_dim.26
  60.7 3.6 all-to-all-start.4
  64.2 1.7 fusion.50
  66.0 1.7 fusion.37
  67.7 7.5 %all-to-all-done.4 = f32[16,32,150]{2,1,0:T(8,128)S(1)} async-done(((f32[16,32,150]{2,1,0:T(8,128)}), f32[16,32,150]{2,1,0:T(8,128)S(1)}, u32[]{:S(2)}, u32[]{:S(2)}) %all-to-all-start.4) | async-done | bytes 307232 | tf_op jit(solution)/shard_map/all_to_all | solution.py:39
  75.4 2.0 convolution_bitcast_fusion
  78.0 1.0 copy-done.2
  79.0 1.1 fusion.31
  80.1 2.3 reshape.42
  82.3 17.0 %all_to_all.41 = f32[16,2,4800]{2,1,0:T(2,128)} all-to-all(f32[16,2,4800]{2,1,0:T(2,128)} %reshape.42), channel_id=1, replica_groups=mesh['replica'=16,'mp'=16] {'mp'}, dimensions={0} | all-to-all | bytes 1228800 | tf_op jit(solution)/shard_map/all_to_all | solution.py:91
  99.4 1.3 reduce_sum.32
  100.8 23.7 %all_to_all.42 = f32[16,2,4800]{2,1,0:T(2,128)} all-to-all(f32[16,2,4800]{2,1,0:T(2,128)S(1)} %broadcast_in_dim.27), channel_id=1, replica_groups=mesh['replica'=16,'mp'=16] {'replica'}, dimensions={0} | all-to-all | bytes 1228800 | tf_op jit(solution)/shard_map/all_to_all | solution.py:39
  124.5 1.3 reduce_sum.33
  125.8 1.0 broadcast_in_dim.28
  126.8 4.3 all-to-all-start.7
  131.0 1.9 slice.115
  132.9 2.1 copy.44
  135.1 9.2 %all-to-all-done.7 = f32[16,2,4800]{2,1,0:T(2,128)} async-done(((f32[16,2,4800]{2,1,0:T(2,128)}), f32[16,2,4800]{2,1,0:T(2,128)}, u32[]{:S(2)}, u32[]{:S(2)}) %all-to-all-start.7) | async-done | bytes 614432 | tf_op jit(solution)/shard_map/all_to_all | solution.py:39
  144.2 5.6 %stack.4 = bf16[16,128,2304]{2,1,0:T(8,128)(2,1)} broadcast(bf16[128,2304]{1,0:T(8,128)(2,1)} %copy.44), dimensions={1,2} | broadcast | bytes 10027008 | tf_op jit(solution)/shard_map/stack | solution.py:54
  149.9 4.8 all-to-all-start
  154.7 2.0 slice.117
  156.6 138.3 %all-to-all-done = bf16[16,128,2304]{2,1,0:T(8,128)(2,1)} async-done(((bf16[16,128,2304]{2,1,0:T(8,128)(2,1)}), bf16[16,128,2304]{2,1,0:T(8,128)(2,1)}, u32[]{:S(2)}, u32[]{:S(2)}) %all-to-all-start) | async-done | bytes 9437216 | tf_op jit(solution)/shard_map/all_to_all | solution.py:54
  294.9 6.9 %stack.5 = bf16[16,128,2496]{1,2,0:T(8,128)(2,1)} broadcast(bf16[128,2496]{0,1:T(8,128)(2,1)} %slice.117), dimensions={1,2} | broadcast | bytes 10862592 | tf_op jit(solution)/shard_map/stack | solution.py:54
  301.9 5.0 %all-to-all-start.1 = ((bf16[16,128,2496]{1,2,0:T(8,128)(2,1)}), bf16[16,128,2496]{1,2,0:T(8,128)(2,1)}, u32[]{:S(2)}, u32[]{:S(2)}) async-start(bf16[16,128,2496]{1,2,0:T(8,128)(2,1)} %stack.5), calls=%async_computation.1 | async-start | bytes 20447232 | tf_op jit(solution)/shard_map/all_to_all | solution.py:54
  306.9 1.8 copy.75
  309.3 2.9 cholesky.17
  312.3 0.6 compare_reduce_fusion
  312.9 0.7 fusion.66
  313.6 2.4 custom-call.7
  316.4 1.6 reshape.43
  318.0 1.5 fusion.29
  319.5 5.9 %convolution_add_fusion = f32[150,2304]{1,0:T(8,128)S(1)} fusion(bf16[2048,2304]{1,0:T(8,128)(2,1)} %bitcast, f32[150,4800]{1,0:T(8,128)} %bitcast.59, bf16[150,2048]{1,0:T(8,128)(2,1)S(1)} %copy-done.7), kind=kOutput, calls=%fused_computation.4 | convolution fusion | flops 1418995200 | bytes 12816384 | tf_op jit(solution)/shard_map/dot_general | solution.py:29
  325.8 7.1 %fusion.24 = f32[150,2048]{1,0:T(8,128)S(1)} fusion(bf16[2048,2304]{1,0:T(8,128)(2,1)} %bitcast, bf16[150,4800]{1,0:T(8,128)(2,1)} %param.7), kind=kOutput, calls=%fused_computation.56 | convolution fusion | flops 1415577600 | bytes 11366400 | tf_op jit(solution)/shard_map/dot_general | solution.py:29
  332.9 122.4 %all-to-all-done.1 = bf16[16,128,2496]{1,2,0:T(8,128)(2,1)} async-done(((bf16[16,128,2496]{1,2,0:T(8,128)(2,1)}), bf16[16,128,2496]{1,2,0:T(8,128)(2,1)}, u32[]{:S(2)}, u32[]{:S(2)}) %all-to-all-start.1) | async-done | bytes 10223648 | tf_op jit(solution)/shard_map/all_to_all | solution.py:54
  455.3 13.7 %copy.45 = bf16[16,128,2496]{2,1,0:T(8,128)(2,1)} copy(bf16[16,128,2496]{1,2,0:T(8,128)(2,1)} %all-to-all-done.1) | data formatting | bytes 20447232 | tf_op jit(solution)/shard_map/all_to_all | solution.py:54
  469.0 6.6 %convolution_add_fusion.1 = f32[150,2496]{1,0:T(8,128)S(1)} fusion(bf16[2048,2496]{1,0:T(8,128)(2,1)} %bitcast.57, f32[150,4800]{1,0:T(8,128)} %bitcast.60, bf16[150,2048]{1,0:T(8,128)(2,1)} %param.5), kind=kOutput, calls=%fused_computation.5 | convolution fusion | flops 1536988800 | bytes 13833216 | tf_op jit(solution)/shard_map/dot_general | solution.py:29
  475.6 0.9 copy-done.1
  477.1 4.8 fusion.5
  482.6 4.6 copy.52
  (55 shorter events, 5.0 us)
Async XLA Ops:
  0.6 1.4 copy-start.6
  1.9 1.5 copy-start.4
  2.2 1.7 copy-start.10
  2.2 1.7 copy-start.12
  4.4 9.0 %copy-start = (f32[1,150,4800]{2,0,1:T(1,128)S(1)}, f32[1,150,4800]{2,0,1:T(1,128)}, u32[]{:S(2)}) copy-start(f32[1,150,4800]{2,0,1:T(1,128)} %param.8) | copy-start | bytes 8640004
  5.6 23.8 %all-to-all-start.2 = ((bf16[16,256,128]{2,1,0:T(8,128)(2,1)}), bf16[16,256,128]{2,1,0:T(8,128)(2,1)}, u32[]{:S(2)}, u32[]{:S(2)}) async-start(bf16[16,256,128]{2,1,0:T(8,128)(2,1)} %copy.46), calls=%async_computation.2 | async-start | bytes 2097152 | tf_op jit(solution)/shard_map/all_to_all | solution.py:68
  13.4 1.7 copy-start.11
  13.4 1.7 copy-start.13
  60.7 14.6 %all-to-all-start.4 = ((f32[16,32,150]{2,1,0:T(8,128)}), f32[16,32,150]{2,1,0:T(8,128)S(1)}, u32[]{:S(2)}, u32[]{:S(2)}) async-start(f32[16,32,150]{2,1,0:T(8,128)} %broadcast_in_dim.26), calls=%async_computation.4 | async-start | bytes 1048576 | tf_op jit(solution)/shard_map/all_to_all | solution.py:39
  75.4 2.0 copy-start.5
  75.4 2.6 copy-start.3
  77.5 1.5 copy-start.2
  126.8 17.5 %all-to-all-start.7 = ((f32[16,2,4800]{2,1,0:T(2,128)}), f32[16,2,4800]{2,1,0:T(2,128)}, u32[]{:S(2)}, u32[]{:S(2)}) async-start(f32[16,2,4800]{2,1,0:T(2,128)} %broadcast_in_dim.28), calls=%async_computation.7 | async-start | bytes 1245184 | tf_op jit(solution)/shard_map/all_to_all | solution.py:39
  149.9 145.1 %all-to-all-start = ((bf16[16,128,2304]{2,1,0:T(8,128)(2,1)}), bf16[16,128,2304]{2,1,0:T(8,128)(2,1)}, u32[]{:S(2)}, u32[]{:S(2)}) async-start(bf16[16,128,2304]{2,1,0:T(8,128)(2,1)} %stack.4), calls=%async_computation | async-start | bytes 18874368 | tf_op jit(solution)/shard_map/all_to_all | solution.py:54
  301.9 153.4 %all-to-all-start.1 = ((bf16[16,128,2496]{1,2,0:T(8,128)(2,1)}), bf16[16,128,2496]{1,2,0:T(8,128)(2,1)}, u32[]{:S(2)}, u32[]{:S(2)}) async-start(bf16[16,128,2496]{1,2,0:T(8,128)(2,1)} %stack.5), calls=%async_computation.1 | async-start | bytes 20447232 | tf_op jit(solution)/shard_map/all_to_all | solution.py:54
  316.4 3.1 copy-start.7
  469.0 7.6 %copy-start.1 = (bf16[16,128,2496]{2,1,0:T(8,128)(2,1)S(1)}, bf16[16,128,2496]{2,1,0:T(8,128)(2,1)}, u32[]{:S(2)}) copy-start(bf16[16,128,2496]{2,1,0:T(8,128)(2,1)} %copy.45) | copy-start | bytes 30670852
  469.0 7.7 %copy-start.8 = (bf16[150,2048]{1,0:T(8,128)(2,1)S(1)}, bf16[150,2048]{1,0:T(8,128)(2,1)}, u32[]{:S(2)}) copy-start(bf16[150,2048]{1,0:T(8,128)(2,1)} %param.5) | copy-start | bytes 1843204
  469.0 8.1 %copy-start.9 = (bf16[150,4800]{1,0:T(8,128)(2,1)S(1)}, bf16[150,4800]{1,0:T(8,128)(2,1)}, u32[]{:S(2)}) copy-start(bf16[150,4800]{1,0:T(8,128)(2,1)} %param.7) | copy-start | bytes 4320004
